TPU v7x, 512 devices: a whole 4x8x8 slice. The times are simulated.
512 devices in a mesh: seq: 64 (over x, y, core), head: 8 (over z).
Axes of the slice: x: 4, y: 8, z: 8, core: 2. Of those that a mesh axis runs over, the one named last changes fastest.
Arguments:
- query_rows: bfloat16 [32768, 1024], P(('seq', 'head')), may hold values from -16 to 16
- key_rows: bfloat16 [32768, 1024], P(('seq', 'head')), may hold values from -16 to 16
- value_rows: bfloat16 [32768, 1024], P(('seq', 'head')), may hold values from -6 to 6
- out_grad: bfloat16 [32768, 1024], P(('seq', 'head')), may hold values from -6 to 6
- random_blocks: int32 [512, 2], P('seq'), may hold values from 0 to 511, as said below
- global_blocks: int32 [2], replicated, may hold values from 0 to 511
Outputs:
- attn_out: bfloat16 [32768, 1024], P(('seq', 'head'))
- q_grad: bfloat16 [32768, 1024], P(('seq', 'head'))
- k_grad: bfloat16 [32768, 1024], P(('seq', 'head'))
- v_grad: bfloat16 [32768, 1024], P(('seq', 'head'))
Inputs may be any that keep to these rules, and one draw needn't show every extreme that they name: `random_blocks`: the 16 random blocks named by the query blocks of one device belong to 16 different devices along `seq`: at most one of them lies among any one device's 8 blocks.
All inputs are finite; a program needn't handle non-finite values.
Results may differ from a plain program's by a relative error of at most 0.011.
Values may be sent and summed in bfloat16 or wider, within the bound.
No kernel may reach another device: no remote copies, remote signals or barrier semaphores. Data moves between devices by JAX's collectives and lax.ppermute only.
A program may use at most 64 MiB of HBM per device.

v0:
```python
from functools import partial
import jax
import jax.numpy as jnp
from jax import lax
from jax.sharding import PartitionSpec as P

HEAD_DIM = 64
BLOCK = 64
RANDOM = 2
GLOBALS = 2
masked_score = -1e30


def extended(x, sides, width):
    for axis, dim in sides:
        peers, length = (lax.axis_size(axis), x.shape[dim])
        up = [(i, (i + 1) % peers) for i in range(peers - 1)]
        down = [(j, i) for i, j in up]
        last = lax.slice_in_dim(x, length - width, length, axis=dim)
        initial = lax.slice_in_dim(x, 0, width, axis=dim)
        before = lax.ppermute(last, axis, up)
        after = lax.ppermute(initial, axis, down)
        x = jnp.concatenate([before, x, after], axis=dim)
    return x


def broadcast(value, axis, source):
    kept = jnp.where(lax.axis_index(axis) == source, value, 0).astype(value.dtype)
    return lax.psum(kept, axis)


def shifted(value, axis, steps):
    count = lax.axis_size(axis)
    initial, last = (max(0, -steps), min(count, count - steps))
    return lax.ppermute(value, axis, [(source, source + steps) for source in range(initial, last)])


def slot_table(flat_ids, per_device, capacity):
    source = flat_ids // per_device
    within = flat_ids % per_device
    order = jnp.arange(flat_ids.shape[0], dtype=jnp.int32)
    earlier = (source[:, None] == source[None, :]) & (order[None, :] < order[:, None])
    rank = jnp.sum(earlier.astype(jnp.int32), axis=1)
    return (source * capacity + rank, within)


def attend_group(packed, scale_factor, width_here):
    query_group, pair_all, grad_group, key_ok = packed
    groups, block_rows = (query_group.shape[0], query_group.shape[1])
    key_count = pair_all.shape[1]
    head_count = width_here // HEAD_DIM
    query_heads = query_group.reshape(groups, block_rows, head_count, HEAD_DIM)
    grad_heads = grad_group.reshape(groups, block_rows, head_count, HEAD_DIM)
    key_heads = pair_all[:, :, :width_here].reshape(groups, key_count, head_count, HEAD_DIM)
    value_heads = pair_all[:, :, width_here:].reshape(groups, key_count, head_count, HEAD_DIM)
    scores = (
        jnp.einsum("gqhd,gkhd->ghqk", query_heads, key_heads, preferred_element_type=jnp.float32)
        * scale_factor
    )
    scores = jnp.where(key_ok[:, None, None, :], scores, masked_score)
    row_max = jnp.max(scores, axis=-1, keepdims=True)
    weights_raw = jnp.exp(scores - row_max)
    probabilities = weights_raw / jnp.sum(weights_raw, axis=-1, keepdims=True)
    probs_half = probabilities.astype(jnp.bfloat16)
    attended = jnp.einsum(
        "ghqk,gkhd->gqhd", probs_half, value_heads, preferred_element_type=jnp.float32
    )
    prob_grad = jnp.einsum(
        "gqhd,gkhd->ghqk", grad_heads, value_heads, preferred_element_type=jnp.float32
    )
    row_delta = jnp.sum(grad_heads.astype(jnp.float32) * attended, axis=-1).transpose(0, 2, 1)[
        ..., None
    ]
    score_grad = (probabilities * (prob_grad - row_delta)).astype(jnp.bfloat16)
    query_grad = (
        jnp.einsum("ghqk,gkhd->gqhd", score_grad, key_heads, preferred_element_type=jnp.float32)
        * scale_factor
    )
    key_grad = (
        jnp.einsum("ghqk,gqhd->gkhd", score_grad, query_heads, preferred_element_type=jnp.float32)
        * scale_factor
    )
    value_grad = jnp.einsum(
        "ghqk,gqhd->gkhd", probs_half, grad_heads, preferred_element_type=jnp.float32
    )
    pair_grad = jnp.concatenate(
        [
            key_grad.reshape(groups, key_count, width_here),
            value_grad.reshape(groups, key_count, width_here),
        ],
        axis=-1,
    )
    pair_grad = pair_grad.reshape(groups, key_count // block_rows, block_rows, 2 * width_here)
    window_part = pair_grad[:, 0:3]
    random_part = pair_grad[:, 3 : 3 + RANDOM].astype(jnp.bfloat16)
    global_part = jnp.sum(pair_grad[:, 3 + RANDOM :], axis=0)
    attended_half = attended.reshape(groups, block_rows, width_here).astype(jnp.bfloat16)
    query_half = query_grad.reshape(groups, block_rows, width_here).astype(jnp.bfloat16)
    return (attended_half, query_half, window_part, random_part, global_part)


def body(query_rows, key_rows, value_rows, out_grad, random_blocks, global_blocks):
    query_here, key_here, value_here, grad_here = (
        lax.all_to_all(query_rows, "head", split_axis=1, concat_axis=0, tiled=True),
        lax.all_to_all(key_rows, "head", split_axis=1, concat_axis=0, tiled=True),
        lax.all_to_all(value_rows, "head", split_axis=1, concat_axis=0, tiled=True),
        lax.all_to_all(out_grad, "head", split_axis=1, concat_axis=0, tiled=True),
    )
    tokens_here, width_here = query_here.shape
    blocks_here = tokens_here // BLOCK
    seq_devices = lax.axis_size("seq")
    my_index = lax.axis_index("seq")
    capacity = max(1, RANDOM * blocks_here // seq_devices)
    slot_total = seq_devices * capacity
    request_total = RANDOM * blocks_here
    scale_factor = HEAD_DIM ** (-0.5)
    pair_rows = jnp.concatenate([key_here, value_here], axis=1)
    pair_blocks = pair_rows.reshape(blocks_here, BLOCK, 2 * width_here)
    padded = extended(pair_rows, (("seq", 0),), BLOCK)
    padded_blocks = padded.reshape(blocks_here + 2, BLOCK, 2 * width_here)
    window_rows = jnp.stack(
        [
            padded_blocks[0:blocks_here],
            padded_blocks[1 : blocks_here + 1],
            padded_blocks[2 : blocks_here + 2],
        ],
        axis=1,
    )
    flat_ids = random_blocks.reshape(request_total)
    slot_of, within_of = slot_table(flat_ids, blocks_here, capacity)
    slot_iota = jnp.arange(slot_total, dtype=jnp.int32)
    slot_hit = slot_of[:, None] == slot_iota[None, :]
    asked_for = jnp.sum(jnp.where(slot_hit, within_of[:, None], 0), axis=0).reshape(
        seq_devices, capacity
    )
    served = lax.all_to_all(asked_for, "seq", split_axis=0, concat_axis=0, tiled=True)
    served_flat = served.reshape(slot_total)
    outgoing = jnp.take(pair_blocks, served_flat, axis=0).reshape(
        seq_devices, capacity, BLOCK, 2 * width_here
    )
    incoming = lax.all_to_all(outgoing, "seq", split_axis=0, concat_axis=0, tiled=True).reshape(
        slot_total, BLOCK, 2 * width_here
    )
    picked = jnp.take(incoming, slot_of, axis=0).reshape(blocks_here, RANDOM, BLOCK, 2 * width_here)
    owners = global_blocks // blocks_here
    owned_at = global_blocks % blocks_here
    fetched = []
    for global_slot in range(GLOBALS):
        piece = lax.dynamic_index_in_dim(pair_blocks, owned_at[global_slot], 0, keepdims=False)
        fetched.append(broadcast(piece, "seq", owners[global_slot]))
    global_pair = jnp.stack(fetched, axis=0)
    global_every = jnp.broadcast_to(
        global_pair[None], (blocks_here, GLOBALS, BLOCK, 2 * width_here)
    )
    pair_all = jnp.concatenate([window_rows, picked, global_every], axis=1).reshape(
        blocks_here, -1, 2 * width_here
    )
    block_number = my_index * blocks_here + jnp.arange(blocks_here, dtype=jnp.int32)
    total_blocks = blocks_here * seq_devices
    part_ok = jnp.ones((blocks_here, 3 + RANDOM + GLOBALS), jnp.bool_)
    part_ok = part_ok.at[:, 0].set(block_number > 0).at[:, 2].set(block_number < total_blocks - 1)
    key_ok = jnp.repeat(part_ok, BLOCK, axis=1)
    group_size = min(blocks_here, max(1, 512 // BLOCK))
    group_count = blocks_here // group_size

    def regroup(tensor):
        return tensor.reshape((group_count, group_size) + tensor.shape[1:])

    packed = (
        regroup(query_here.reshape(blocks_here, BLOCK, width_here)),
        regroup(pair_all),
        regroup(grad_here.reshape(blocks_here, BLOCK, width_here)),
        regroup(key_ok),
    )
    attended, query_grad, window_grad, random_grad, global_grad = lax.map(
        partial(attend_group, scale_factor=scale_factor, width_here=width_here), packed
    )
    attended = attended.reshape(tokens_here, width_here)
    query_grad = query_grad.reshape(tokens_here, width_here)
    window_grad = window_grad.reshape(blocks_here, 3, BLOCK, 2 * width_here)
    window_sum = (
        jnp.pad(window_grad[:, 0], ((0, 2), (0, 0), (0, 0)))
        + jnp.pad(window_grad[:, 1], ((1, 1), (0, 0), (0, 0)))
        + jnp.pad(window_grad[:, 2], ((2, 0), (0, 0), (0, 0)))
    )
    from_above = shifted(window_sum[0].astype(jnp.bfloat16), "seq", -1).astype(jnp.float32)
    from_below = shifted(window_sum[blocks_here + 1].astype(jnp.bfloat16), "seq", 1).astype(
        jnp.float32
    )
    owned_grad = window_sum[1 : blocks_here + 1]
    owned_grad = owned_grad.at[blocks_here - 1].add(from_above).at[0].add(from_below)
    random_flat = random_grad.reshape(request_total, BLOCK, 2 * width_here)
    slot_used = jnp.any(slot_hit, axis=0)
    source_request = jnp.sum(
        jnp.where(slot_hit, jnp.arange(request_total, dtype=jnp.int32)[:, None], 0), axis=0
    )
    sending = jnp.where(
        slot_used[:, None, None],
        jnp.take(random_flat, source_request, axis=0),
        jnp.zeros((), jnp.bfloat16),
    )
    sending = sending.reshape(seq_devices, capacity, BLOCK, 2 * width_here)
    returned = lax.all_to_all(sending, "seq", split_axis=0, concat_axis=0, tiled=True).reshape(
        slot_total, BLOCK * 2 * width_here
    )
    owner_hit = (served_flat[None, :] == jnp.arange(blocks_here, dtype=jnp.int32)[:, None]).astype(
        jnp.bfloat16
    )
    owned_grad = owned_grad + jnp.dot(
        owner_hit, returned, preferred_element_type=jnp.float32
    ).reshape(blocks_here, BLOCK, 2 * width_here)
    global_total = lax.psum(jnp.sum(global_grad, axis=0), "seq")
    block_iota = jnp.arange(blocks_here, dtype=jnp.int32)
    for global_slot in range(GLOBALS):
        hit_mask = (block_iota == owned_at[global_slot]) & (owners[global_slot] == my_index)
        owned_grad = owned_grad + jnp.where(
            hit_mask[:, None, None], global_total[global_slot][None], 0.0
        )
    pair_grad = owned_grad.reshape(tokens_here, 2 * width_here).astype(jnp.bfloat16)
    return (
        lax.all_to_all(attended, "head", split_axis=0, concat_axis=1, tiled=True),
        lax.all_to_all(query_grad, "head", split_axis=0, concat_axis=1, tiled=True),
        lax.all_to_all(pair_grad[:, :width_here], "head", split_axis=0, concat_axis=1, tiled=True),
        lax.all_to_all(pair_grad[:, width_here:], "head", split_axis=0, concat_axis=1, tiled=True),
    )


def solution(mesh):
    placed = (
        P(("seq", "head"), None),
        P(("seq", "head"), None),
        P(("seq", "head"), None),
        P(("seq", "head"), None),
        P("seq", None),
        P(),
    )
    return jax.shard_map(
        body,
        mesh=mesh,
        in_specs=placed,
        out_specs=(
            P(("seq", "head"), None),
            P(("seq", "head"), None),
            P(("seq", "head"), None),
            P(("seq", "head"), None),
        ),
        check_vma=False,
    )
```

profile of v0, /device:TPU:2, one launch (start us, length us, event | category | flops | bytes accessed | tf_op | source)
XLA Modules:
  0.0 583.4 jit_solution(378194306207217572)
XLA Ops:
  9.1 10.7 %all-to-all-start.2 = ((s32[64,1,1]{2,1,0:T(1,128)}), s32[64,1,1]{2,1,0:T(1,128)S(1)}, u32[]{:S(2)}, u32[]{:S(2)}) async-start(s32[64,1,1]{2,1,0:T(1,128)} %copy.164), calls=%async_computation.2 | async-start | bytes 65536 | tf_op jit(solution)/shard_map/all_to_all | solution.py:136
  23.6 4.7 all-to-all-done.2
  28.2 10.3 %all-to-all-start = ((bf16[64,8,128]{2,0,1:T(8,128)(2,1)}), bf16[64,8,128]{2,0,1:T(8,128)(2,1)S(1)}, u32[]{:S(2)}, u32[]{:S(2)}) async-start(bf16[64,8,128]{2,0,1:T(8,128)(2,1)} %copy_bitcast_fusion.7), calls=%async_computation | async-start | bytes 262144 | tf_op jit(solution)/shard_map/all_to_all | solution.py:105
  41.4 6.3 %all-to-all-done = bf16[64,8,128]{2,0,1:T(8,128)(2,1)S(1)} async-done(((bf16[64,8,128]{2,0,1:T(8,128)(2,1)}), bf16[64,8,128]{2,0,1:T(8,128)(2,1)S(1)}, u32[]{:S(2)}, u32[]{:S(2)}) %all-to-all-start) | async-done | bytes 131104 | tf_op jit(solution)/shard_map/all_to_all | solution.py:105
  47.7 3.4 all-to-all-start.1
  51.1 9.0 %all-to-all-done.1 = bf16[64,8,128]{2,0,1:T(8,128)(2,1)S(1)} async-done(((bf16[64,8,128]{2,0,1:T(8,128)(2,1)}), bf16[64,8,128]{2,0,1:T(8,128)(2,1)S(1)}, u32[]{:S(2)}, u32[]{:S(2)}) %all-to-all-start.1) | async-done | bytes 131104 | tf_op jit(solution)/shard_map/all_to_all | solution.py:106
  60.0 3.4 all-to-all-start.4
  64.2 8.2 %all-to-all-done.4 = bf16[64,8,128]{2,0,1:T(8,128)(2,1)S(1)} async-done(((bf16[64,8,128]{2,0,1:T(8,128)(2,1)}), bf16[64,8,128]{2,0,1:T(8,128)(2,1)S(1)}, u32[]{:S(2)}, u32[]{:S(2)}) %all-to-all-start.4) | async-done | bytes 131104 | tf_op jit(solution)/shard_map/all_to_all | solution.py:104
  72.4 3.4 all-to-all-start.6
  77.4 7.4 %all-to-all-done.6 = bf16[64,8,128]{2,0,1:T(8,128)(2,1)S(1)} async-done(((bf16[64,8,128]{2,0,1:T(8,128)(2,1)}), bf16[64,8,128]{2,0,1:T(8,128)(2,1)S(1)}, u32[]{:S(2)}, u32[]{:S(2)}) %all-to-all-start.6) | async-done | bytes 131104 | tf_op jit(solution)/shard_map/all_to_all | solution.py:107
  84.8 6.0 %all-to-all-start.3 = ((bf16[64,1,64,256]{3,2,1,0:T(8,128)(2,1)}), bf16[64,1,64,256]{3,2,1,0:T(8,128)(2,1)S(1)}, u32[]{:S(2)}, u32[]{:S(2)}) async-start(bf16[64,1,64,256]{3,2,1,0:T(8,128)(2,1)} %fusion.9), calls=%async_computation.3 | async-start | bytes 4194304 | tf_op jit(solution)/shard_map/all_to_all | solution.py:141
  100.8 4.3 collective-permute-start.1
  107.9 170.9 %all-reduce.10.cloned.1.call-done = (bf16[1,64,256]{2,1,0:T(8,128)(2,1)}, bf16[1,64,256]{2,1,0:T(8,128)(2,1)}) async-done(((bf16[1,64,256]{2,1,0:T(8,128)(2,1)}, bf16[1,64,256]{2,1,0:T(8,128)(2,1)}), (bf16[1,64,256]{2,1,0:T(8,128)(2,1)}, bf16[1,64,256]{2,1,0:T(8,128)(2,1)})) %all-reduce.10.cloned.1.call-update) | async-done | bytes 65552 | tf_op jit(solution)/shard_map/psum | solution.py:29
  294.6 7.4 %all-to-all-start.5 = ((bf16[8,64,128]{2,1,0:T(8,128)(2,1)}), bf16[8,64,128]{2,1,0:T(8,128)(2,1)}, u32[]{:S(2)}, u32[]{:S(2)}) async-start(bf16[8,64,128]{2,1,0:T(8,128)(2,1)} %copy.174), calls=%async_computation.5 | async-start | bytes 262144 | tf_op jit(solution)/shard_map/all_to_all | solution.py:221
  307.6 4.5 reshape.553
  312.0 3.7 copy.185
  322.1 7.1 %all-to-all-start.8 = ((bf16[64,1,64,256]{3,2,1,0:T(8,128)(2,1)}), bf16[64,1,64,256]{3,2,1,0:T(8,128)(2,1)}, u32[]{:S(2)}, u32[]{:S(2)}) async-start(bf16[64,1,64,256]{3,2,1,0:T(8,128)(2,1)} %fusion.5), calls=%async_computation.8 | async-start | bytes 4194304 | tf_op jit(solution)/shard_map/all_to_all | solution.py:203
  334.7 4.3 collective-permute-start.2
  345.8 27.7 %collective-permute-done.2 = bf16[64,256]{1,0:T(8,128)(2,1)} collective-permute-done((bf16[64,256]{1,0:T(8,128)(2,1)}, bf16[64,256]{1,0:T(8,128)(2,1)}, u32[]{:S(2)}, u32[]{:S(2)}) %collective-permute-start.2) | collective-permute-done | bytes 32800 | tf_op jit(solution)/shard_map/ppermute | solution.py:35
  378.2 152.1 %all-reduce.8.cloned.1.call-done = f32[2,64,256]{2,1,0:T(8,128)} async-done(((f32[2,64,256]{2,1,0:T(8,128)}), f32[2,64,256]{2,1,0:T(8,128)}) %all-reduce.8.cloned.1.call-update) | async-done | bytes 131088 | tf_op jit(solution)/shard_map/psum | solution.py:212
  532.8 7.4 %all-to-all-start.7 = ((bf16[8,64,128]{2,1,0:T(8,128)(2,1)}), bf16[8,64,128]{2,1,0:T(8,128)(2,1)S(1)}, u32[]{:S(2)}, u32[]{:S(2)}) async-start(bf16[8,64,128]{2,1,0:T(8,128)(2,1)} %copy.179), calls=%async_computation.7 | async-start | bytes 262144 | tf_op jit(solution)/shard_map/all_to_all | solution.py:222
  543.8 6.8 %all-to-all-done.7 = bf16[8,64,128]{2,1,0:T(8,128)(2,1)S(1)} async-done(((bf16[8,64,128]{2,1,0:T(8,128)(2,1)}), bf16[8,64,128]{2,1,0:T(8,128)(2,1)S(1)}, u32[]{:S(2)}, u32[]{:S(2)}) %all-to-all-start.7) | async-done | bytes 131104 | tf_op jit(solution)/shard_map/all_to_all | solution.py:222
  554.7 8.9 %all-to-all-done.9 = bf16[8,64,128]{2,1,0:T(8,128)(2,1)S(1)} async-done(((bf16[8,64,128]{2,1,0:T(8,128)(2,1)}), bf16[8,64,128]{2,1,0:T(8,128)(2,1)S(1)}, u32[]{:S(2)}, u32[]{:S(2)}) %all-to-all-start.9) | async-done | bytes 131104 | tf_op jit(solution)/shard_map/all_to_all | solution.py:223
  567.6 8.3 %all-to-all-done.10 = bf16[8,64,128]{2,1,0:T(8,128)(2,1)S(1)} async-done(((bf16[8,64,128]{2,1,0:T(8,128)(2,1)}), bf16[8,64,128]{2,1,0:T(8,128)(2,1)S(1)}, u32[]{:S(2)}, u32[]{:S(2)}) %all-to-all-start.10) | async-done | bytes 131104 | tf_op jit(solution)/shard_map/all_to_all | solution.py:224
  (124 shorter events, 76.4 us)
Async XLA Ops:
  7.2 12.6 %copy-start = (bf16[64,1024]{1,0:T(8,128)(2,1)S(1)}, bf16[64,1024]{1,0:T(8,128)(2,1)}, u32[]{:S(2)}) copy-start(bf16[64,1024]{1,0:T(8,128)(2,1)} %param.14) | copy-start | bytes 393220
  9.1 19.2 %all-to-all-start.2 = ((s32[64,1,1]{2,1,0:T(1,128)}), s32[64,1,1]{2,1,0:T(1,128)S(1)}, u32[]{:S(2)}, u32[]{:S(2)}) async-start(s32[64,1,1]{2,1,0:T(1,128)} %copy.164), calls=%async_computation.2 | async-start | bytes 65536 | tf_op jit(solution)/shard_map/all_to_all | solution.py:136
  28.2 19.4 %all-to-all-start = ((bf16[64,8,128]{2,0,1:T(8,128)(2,1)}), bf16[64,8,128]{2,0,1:T(8,128)(2,1)S(1)}, u32[]{:S(2)}, u32[]{:S(2)}) async-start(bf16[64,8,128]{2,0,1:T(8,128)(2,1)} %copy_bitcast_fusion.7), calls=%async_computation | async-start | bytes 262144 | tf_op jit(solution)/shard_map/all_to_all | solution.py:105
  47.7 12.4 %all-to-all-start.1 = ((bf16[64,8,128]{2,0,1:T(8,128)(2,1)}), bf16[64,8,128]{2,0,1:T(8,128)(2,1)S(1)}, u32[]{:S(2)}, u32[]{:S(2)}) async-start(bf16[64,8,128]{2,0,1:T(8,128)(2,1)} %copy_bitcast_fusion.6), calls=%async_computation.1 | async-start | bytes 262144 | tf_op jit(solution)/shard_map/all_to_all | solution.py:106
  60.0 12.4 %all-to-all-start.4 = ((bf16[64,8,128]{2,0,1:T(8,128)(2,1)}), bf16[64,8,128]{2,0,1:T(8,128)(2,1)S(1)}, u32[]{:S(2)}, u32[]{:S(2)}) async-start(bf16[64,8,128]{2,0,1:T(8,128)(2,1)} %copy_bitcast_fusion.5), calls=%async_computation.4 | async-start | bytes 262144 | tf_op jit(solution)/shard_map/all_to_all | solution.py:104
  72.4 12.4 %all-to-all-start.6 = ((bf16[64,8,128]{2,0,1:T(8,128)(2,1)}), bf16[64,8,128]{2,0,1:T(8,128)(2,1)S(1)}, u32[]{:S(2)}, u32[]{:S(2)}) async-start(bf16[64,8,128]{2,0,1:T(8,128)(2,1)} %copy_bitcast_fusion.4), calls=%async_computation.6 | async-start | bytes 262144 | tf_op jit(solution)/shard_map/all_to_all | solution.py:107
  77.4 13.4 %copy-start.10 = (s32[2]{0:T(128)S(1)}, s32[2]{0:T(128)}, u32[]{:S(2)}) copy-start(s32[2]{0:T(128)} %param.19) | copy-start | bytes 28
  84.8 197.1 %all-to-all-start.3 = ((bf16[64,1,64,256]{3,2,1,0:T(8,128)(2,1)}), bf16[64,1,64,256]{3,2,1,0:T(8,128)(2,1)S(1)}, u32[]{:S(2)}, u32[]{:S(2)}) async-start(bf16[64,1,64,256]{3,2,1,0:T(8,128)(2,1)} %fusion.9), calls=%async_computation.3 | async-start | bytes 4194304 | tf_op jit(solution)/shard_map/all_to_all | solution.py:141
  90.7 188.1 %all-reduce.10.cloned.1.call-start = ((), (), s32[]{:S(2)}) async-start(), calls=%async_computation.12 | async-start | bytes 131072 | tf_op jit(solution)/shard_map/psum | solution.py:29
  100.8 186.2 %copy-start.6 = (bf16[8,64,128]{1,2,0:T(8,128)(2,1)}, bf16[8,64,128]{1,2,0:T(8,128)(2,1)S(1)}, u32[]{:S(2)}) copy-start(bf16[8,64,128]{1,2,0:T(8,128)(2,1)S(1)} %copy.199) | copy-start | bytes 393220
  100.8 178.8 %collective-permute-start.1 = (bf16[64,256]{1,0:T(8,128)(2,1)S(1)}, bf16[64,256]{1,0:T(8,128)(2,1)S(1)}, u32[]{:S(2)}, u32[]{:S(2)}) collective-permute-start(bf16[64,256]{1,0:T(8,128)(2,1)S(1)} %get-tuple-element.103), channel_id=1, source_target_pairs={{8,0},{16,8},{24,16},{32,24},{40,32},{48,40},{56,48},{64,56},{72,6... | collective-permute-start | bytes 98312 | tf_op jit(solution)/shard_map/ppermute | solution.py:22
  105.1 174.5 %collective-permute-start = (bf16[64,256]{1,0:T(8,128)(2,1)S(1)}, bf16[64,256]{1,0:T(8,128)(2,1)S(1)}, u32[]{:S(2)}, u32[]{:S(2)}) collective-permute-start(bf16[64,256]{1,0:T(8,128)(2,1)S(1)} %get-tuple-element.104), channel_id=1, source_target_pairs={{0,8},{8,16},{16,24},{24,32},{32,40},{40,48},{48,56},{56,64},{64,7... | collective-permute-start | bytes 98312 | tf_op jit(solution)/shard_map/ppermute | solution.py:21
  286.9 4.4 copy-start.4
  293.2 8.7 %copy-start.7 = (bf16[8,64,128]{1,2,0:T(8,128)(2,1)S(1)}, bf16[8,64,128]{1,2,0:T(8,128)(2,1)}, u32[]{:S(2)}) copy-start(bf16[8,64,128]{1,2,0:T(8,128)(2,1)} %copy-done.6) | copy-start | bytes 393220
  294.6 27.5 %all-to-all-start.5 = ((bf16[8,64,128]{2,1,0:T(8,128)(2,1)}), bf16[8,64,128]{2,1,0:T(8,128)(2,1)}, u32[]{:S(2)}, u32[]{:S(2)}) async-start(bf16[8,64,128]{2,1,0:T(8,128)(2,1)} %copy.174), calls=%async_computation.5 | async-start | bytes 262144 | tf_op jit(solution)/shard_map/all_to_all | solution.py:221
  322.1 210.7 %all-to-all-start.8 = ((bf16[64,1,64,256]{3,2,1,0:T(8,128)(2,1)}), bf16[64,1,64,256]{3,2,1,0:T(8,128)(2,1)}, u32[]{:S(2)}, u32[]{:S(2)}) async-start(bf16[64,1,64,256]{3,2,1,0:T(8,128)(2,1)} %fusion.5), calls=%async_computation.8 | async-start | bytes 4194304 | tf_op jit(solution)/shard_map/all_to_all | solution.py:203
  329.2 201.2 %all-reduce.8.cloned.1.call-start = ((), (), s32[]{:S(2)}) async-start(), calls=%async_computation.11 | async-start | bytes 262144 | tf_op jit(solution)/shard_map/psum | solution.py:212
  333.1 6.0 %copy-start.2 = (bf16[8,448,128]{1,2,0:T(8,128)(2,1)S(1)}, bf16[8,448,128]{1,2,0:T(8,128)(2,1)}, u32[]{:S(2)}) copy-start(bf16[8,448,128]{1,2,0:T(8,128)(2,1)} %copy-done.1) | copy-start | bytes 2752516
  334.7 38.8 %collective-permute-start.2 = (bf16[64,256]{1,0:T(8,128)(2,1)}, bf16[64,256]{1,0:T(8,128)(2,1)}, u32[]{:S(2)}, u32[]{:S(2)}) collective-permute-start(bf16[64,256]{1,0:T(8,128)(2,1)} %get-tuple-element.96), channel_id=1, source_target_pairs={{8,0},{16,8},{24,16},{32,24},{40,32},{48,40},{56,48},{64,56},{72,6... | collective-permute-start | bytes 98312 | tf_op jit(solution)/shard_map/ppermute | solution.py:35
  340.2 5.5 copy-start.3
  343.8 33.2 %collective-permute-start.3 = (bf16[64,256]{1,0:T(8,128)(2,1)S(1)}, bf16[64,256]{1,0:T(8,128)(2,1)S(1)}, u32[]{:S(2)}, u32[]{:S(2)}) collective-permute-start(bf16[64,256]{1,0:T(8,128)(2,1)S(1)} %copy-done.9), channel_id=1, source_target_pairs={{0,8},{8,16},{16,24},{24,32},{32,40},{40,48},{48,56},{56,64},{64,7... | collective-permute-start | bytes 98312 | tf_op jit(solution)/shard_map/ppermute | solution.py:35
  532.8 17.8 %all-to-all-start.7 = ((bf16[8,64,128]{2,1,0:T(8,128)(2,1)}), bf16[8,64,128]{2,1,0:T(8,128)(2,1)S(1)}, u32[]{:S(2)}, u32[]{:S(2)}) async-start(bf16[8,64,128]{2,1,0:T(8,128)(2,1)} %copy.179), calls=%async_computation.7 | async-start | bytes 262144 | tf_op jit(solution)/shard_map/all_to_all | solution.py:222
  550.6 12.9 %all-to-all-start.9 = ((bf16[8,64,128]{2,1,0:T(8,128)(2,1)}), bf16[8,64,128]{2,1,0:T(8,128)(2,1)S(1)}, u32[]{:S(2)}, u32[]{:S(2)}) async-start(bf16[8,64,128]{2,1,0:T(8,128)(2,1)} %bitcast.56), calls=%async_computation.9 | async-start | bytes 262144 | tf_op jit(solution)/shard_map/all_to_all | solution.py:223
  563.5 12.4 %all-to-all-start.10 = ((bf16[8,64,128]{2,1,0:T(8,128)(2,1)}), bf16[8,64,128]{2,1,0:T(8,128)(2,1)S(1)}, u32[]{:S(2)}, u32[]{:S(2)}) async-start(bf16[8,64,128]{2,1,0:T(8,128)(2,1)} %bitcast.58), calls=%async_computation.10 | async-start | bytes 262144 | tf_op jit(solution)/shard_map/all_to_all | solution.py:224
  (5 other events, 12.5 us)
Sparse Core Ops, SparseCore 0:
  100.7 178.0 all-reduce.9
  343.9 186.4 all-reduce.7
where the time goes:
time: 585 us; the launch traced here: 583 us
  waiting for transfers between devices  413 us (71%)
  starting transfers between devices  78.2 us (13%)
  local copies, waits for them, and re-layouts  40.5 us (7%)
  between operations  21 us (4%)
  other arithmetic  19.5 us (3%)
  matrix products  11.2 us (2%)
    psum x1, waiting for transfers between devices, broadcast(): return lax.psum(kept, axis)  171 us
    psum x1, waiting for transfers between devices, body(): global_total = lax.psum(jnp.sum(global_grad, axis=0), 'seq')  152 us
    ppermute x2, waiting for transfers between devices, shifted(): lax.ppermute(value, axis, [(source, source + steps) for source in range(i...  30.4 us
    concatenate x4, local copies, waits for them, and re-layouts, attend_group(): jnp.concatenate([key_grad.reshape(groups, key_count, width_here), value_g...  13.3 us
  transfers between devices with their start and end apart: 17, of which 12 were waited for; matrix products, arithmetic and copies ran while one was open for 10% of the time, Pallas kernels for 0%

commit v1 on v0

--- a/solution.py
+++ b/solution.py
@@ -209,7 +209,7 @@
     owned_grad = owned_grad + jnp.dot(
         owner_hit, returned, preferred_element_type=jnp.float32
     ).reshape(blocks_here, BLOCK, 2 * width_here)
-    global_total = lax.psum(jnp.sum(global_grad, axis=0), "seq")
+    global_total = jnp.sum(lax.all_gather(jnp.sum(global_grad, axis=0), "seq"), axis=0)
     block_iota = jnp.arange(blocks_here, dtype=jnp.int32)
     for global_slot in range(GLOBALS):
         hit_mask = (block_iota == owned_at[global_slot]) & (owners[global_slot] == my_index)

time: 585 us -> 464 us (0.79)
  the two profiles are of different devices: /device:TPU:2 before, /device:TPU:8 now
where the time goes in v1:
time: 464 us; the launch traced here: 462 us
  waiting for transfers between devices  298 us (64%)
  starting transfers between devices  72.6 us (16%)
  local copies, waits for them, and re-layouts  38.4 us (8%)
  other arithmetic  21.7 us (5%)
  between operations  20.6 us (4%)
  matrix products  11.2 us (2%)
    psum x1, waiting for transfers between devices, broadcast(): return lax.psum(kept, axis)  172 us
    ppermute x2, waiting for transfers between devices, shifted(): lax.ppermute(value, axis, [(source, source + steps) for source in range(i...  46.5 us
    all_gather x1, waiting for transfers between devices, body(): lax.all_gather(jnp.sum(global_grad, axis=0), 'seq')  17.7 us
    concatenate x4, local copies, waits for them, and re-layouts, attend_group(): jnp.concatenate([key_grad.reshape(groups, key_count, width_here), value_g...  13.4 us
    all_to_all x1, starting transfers between devices, body(): lax.all_to_all(asked_for, 'seq', split_axis=0, concat_axis=0, tiled=True)  10.6 us
    all_to_all x1, starting transfers between devices, body(): lax.all_to_all(key_rows, 'head', split_axis=1, concat_axis=0, tiled=True)  10.3 us
  transfers between devices with their start and end apart: 17, of which 12 were waited for; matrix products, arithmetic and copies ran while one was open for 9% of the time, Pallas kernels for 0%

profile of v1, /device:TPU:8, one launch (start us, length us, event | category | flops | bytes accessed | tf_op | source)
XLA Modules:
  0.0 462.0 jit_solution(13066635336618769306)
XLA Ops:
  9.1 10.6 %all-to-all-start.2 = ((s32[64,1,1]{2,1,0:T(1,128)}), s32[64,1,1]{2,1,0:T(1,128)S(1)}, u32[]{:S(2)}, u32[]{:S(2)}) async-start(s32[64,1,1]{2,1,0:T(1,128)} %copy.164), calls=%async_computation.2 | async-start | bytes 65536 | tf_op jit(solution)/shard_map/all_to_all | solution.py:136
  23.5 4.6 %all-to-all-done.2 = s32[64,1,1]{2,1,0:T(1,128)S(1)} async-done(((s32[64,1,1]{2,1,0:T(1,128)}), s32[64,1,1]{2,1,0:T(1,128)S(1)}, u32[]{:S(2)}, u32[]{:S(2)}) %all-to-all-start.2) | async-done | bytes 288 | tf_op jit(solution)/shard_map/all_to_all | solution.py:136
  28.1 10.3 %all-to-all-start = ((bf16[64,8,128]{2,0,1:T(8,128)(2,1)}), bf16[64,8,128]{2,0,1:T(8,128)(2,1)S(1)}, u32[]{:S(2)}, u32[]{:S(2)}) async-start(bf16[64,8,128]{2,0,1:T(8,128)(2,1)} %copy_bitcast_fusion.7), calls=%async_computation | async-start | bytes 262144 | tf_op jit(solution)/shard_map/all_to_all | solution.py:105
  41.2 6.3 %all-to-all-done = bf16[64,8,128]{2,0,1:T(8,128)(2,1)S(1)} async-done(((bf16[64,8,128]{2,0,1:T(8,128)(2,1)}), bf16[64,8,128]{2,0,1:T(8,128)(2,1)S(1)}, u32[]{:S(2)}, u32[]{:S(2)}) %all-to-all-start) | async-done | bytes 131104 | tf_op jit(solution)/shard_map/all_to_all | solution.py:105
  47.5 3.4 all-to-all-start.1
  51.0 9.0 %all-to-all-done.1 = bf16[64,8,128]{2,0,1:T(8,128)(2,1)S(1)} async-done(((bf16[64,8,128]{2,0,1:T(8,128)(2,1)}), bf16[64,8,128]{2,0,1:T(8,128)(2,1)S(1)}, u32[]{:S(2)}, u32[]{:S(2)}) %all-to-all-start.1) | async-done | bytes 131104 | tf_op jit(solution)/shard_map/all_to_all | solution.py:106
  59.9 3.4 all-to-all-start.4
  64.0 8.2 %all-to-all-done.4 = bf16[64,8,128]{2,0,1:T(8,128)(2,1)S(1)} async-done(((bf16[64,8,128]{2,0,1:T(8,128)(2,1)}), bf16[64,8,128]{2,0,1:T(8,128)(2,1)S(1)}, u32[]{:S(2)}, u32[]{:S(2)}) %all-to-all-start.4) | async-done | bytes 131104 | tf_op jit(solution)/shard_map/all_to_all | solution.py:104
  72.3 3.4 all-to-all-start.6
  77.3 7.4 %all-to-all-done.6 = bf16[64,8,128]{2,0,1:T(8,128)(2,1)S(1)} async-done(((bf16[64,8,128]{2,0,1:T(8,128)(2,1)}), bf16[64,8,128]{2,0,1:T(8,128)(2,1)S(1)}, u32[]{:S(2)}, u32[]{:S(2)}) %all-to-all-start.6) | async-done | bytes 131104 | tf_op jit(solution)/shard_map/all_to_all | solution.py:107
  84.7 6.0 %all-to-all-start.3 = ((bf16[64,1,64,256]{3,2,1,0:T(8,128)(2,1)}), bf16[64,1,64,256]{3,2,1,0:T(8,128)(2,1)S(1)}, u32[]{:S(2)}, u32[]{:S(2)}) async-start(bf16[64,1,64,256]{3,2,1,0:T(8,128)(2,1)} %fusion.9), calls=%async_computation.3 | async-start | bytes 4194304 | tf_op jit(solution)/shard_map/all_to_all | solution.py:141
  105.3 171.9 %all-reduce.7.cloned.1.call-done = (bf16[1,64,256]{2,1,0:T(8,128)(2,1)}, bf16[1,64,256]{2,1,0:T(8,128)(2,1)}) async-done(((bf16[1,64,256]{2,1,0:T(8,128)(2,1)}, bf16[1,64,256]{2,1,0:T(8,128)(2,1)}), (bf16[1,64,256]{2,1,0:T(8,128)(2,1)}, bf16[1,64,256]{2,1,0:T(8,128)(2,1)})) %all-reduce.7.cloned.1.call-update) | async-done | bytes 65552 | tf_op jit(solution)/shard_map/psum | solution.py:29
  298.9 4.5 reshape.554
  303.4 3.7 copy.185
  309.8 7.4 %all-to-all-start.5 = ((bf16[8,64,128]{2,1,0:T(8,128)(2,1)}), bf16[8,64,128]{2,1,0:T(8,128)(2,1)}, u32[]{:S(2)}, u32[]{:S(2)}) async-start(bf16[8,64,128]{2,1,0:T(8,128)(2,1)} %copy.174), calls=%async_computation.5 | async-start | bytes 262144 | tf_op jit(solution)/shard_map/all_to_all | solution.py:221
  327.0 7.5 %all-to-all-start.8 = ((bf16[64,1,64,256]{3,2,1,0:T(8,128)(2,1)}), bf16[64,1,64,256]{3,2,1,0:T(8,128)(2,1)}, u32[]{:S(2)}, u32[]{:S(2)}) async-start(bf16[64,1,64,256]{3,2,1,0:T(8,128)(2,1)} %fusion.5), calls=%async_computation.8 | async-start | bytes 4194304 | tf_op jit(solution)/shard_map/all_to_all | solution.py:203
  344.0 46.5 %collective-permute-done.2 = bf16[64,256]{1,0:T(8,128)(2,1)S(1)} collective-permute-done((bf16[64,256]{1,0:T(8,128)(2,1)S(1)}, bf16[64,256]{1,0:T(8,128)(2,1)S(1)}, u32[]{:S(2)}, u32[]{:S(2)}) %collective-permute-start.2) | collective-permute-done | bytes 32800 | tf_op jit(solution)/shard_map/ppermute | solution.py:35
  393.5 17.7 %all-gather.3.cloned.1.call-done = f32[128,64,256]{2,1,0:T(8,128)} async-done(((f32[2,64,256]{2,1,0:T(8,128)}), f32[128,64,256]{2,1,0:T(8,128)}) %all-gather.3.cloned.1.call-update) | async-done | bytes 8388624 | tf_op jit(solution)/shard_map/all_gather | solution.py:212
  411.2 3.9 reduce_sum.85
  415.1 5.1 %all-to-all-start.7 = ((bf16[8,64,128]{2,1,0:T(8,128)(2,1)}), bf16[8,64,128]{2,1,0:T(8,128)(2,1)S(1)}, u32[]{:S(2)}, u32[]{:S(2)}) async-start(bf16[8,64,128]{2,1,0:T(8,128)(2,1)} %copy.179), calls=%async_computation.7 | async-start | bytes 262144 | tf_op jit(solution)/shard_map/all_to_all | solution.py:222
  423.9 5.9 %all-to-all-done.7 = bf16[8,64,128]{2,1,0:T(8,128)(2,1)S(1)} async-done(((bf16[8,64,128]{2,1,0:T(8,128)(2,1)}), bf16[8,64,128]{2,1,0:T(8,128)(2,1)S(1)}, u32[]{:S(2)}, u32[]{:S(2)}) %all-to-all-start.7) | async-done | bytes 131104 | tf_op jit(solution)/shard_map/all_to_all | solution.py:222
  429.7 3.4 all-to-all-start.9
  433.8 8.3 %all-to-all-done.9 = bf16[8,64,128]{2,1,0:T(8,128)(2,1)S(1)} async-done(((bf16[8,64,128]{2,1,0:T(8,128)(2,1)}), bf16[8,64,128]{2,1,0:T(8,128)(2,1)S(1)}, u32[]{:S(2)}, u32[]{:S(2)}) %all-to-all-start.9) | async-done | bytes 131104 | tf_op jit(solution)/shard_map/all_to_all | solution.py:223
  446.2 8.3 %all-to-all-done.10 = bf16[8,64,128]{2,1,0:T(8,128)(2,1)S(1)} async-done(((bf16[8,64,128]{2,1,0:T(8,128)(2,1)}), bf16[8,64,128]{2,1,0:T(8,128)(2,1)S(1)}, u32[]{:S(2)}, u32[]{:S(2)}) %all-to-all-start.10) | async-done | bytes 131104 | tf_op jit(solution)/shard_map/all_to_all | solution.py:224
  (127 shorter events, 74.8 us)
Async XLA Ops:
  7.2 12.5 %copy-start = (bf16[64,1024]{1,0:T(8,128)(2,1)S(1)}, bf16[64,1024]{1,0:T(8,128)(2,1)}, u32[]{:S(2)}) copy-start(bf16[64,1024]{1,0:T(8,128)(2,1)} %param.14) | copy-start | bytes 393220
  8.3 90.7 %copy-start.9 = (s32[64]{0:T(128)}, s32[64]{0:T(128)S(1)}, u32[]{:S(2)}) copy-start(s32[64]{0:T(128)S(1)} %get-tuple-element.82) | copy-start | bytes 772
  9.1 19.1 %all-to-all-start.2 = ((s32[64,1,1]{2,1,0:T(1,128)}), s32[64,1,1]{2,1,0:T(1,128)S(1)}, u32[]{:S(2)}, u32[]{:S(2)}) async-start(s32[64,1,1]{2,1,0:T(1,128)} %copy.164), calls=%async_computation.2 | async-start | bytes 65536 | tf_op jit(solution)/shard_map/all_to_all | solution.py:136
  28.1 19.4 %all-to-all-start = ((bf16[64,8,128]{2,0,1:T(8,128)(2,1)}), bf16[64,8,128]{2,0,1:T(8,128)(2,1)S(1)}, u32[]{:S(2)}, u32[]{:S(2)}) async-start(bf16[64,8,128]{2,0,1:T(8,128)(2,1)} %copy_bitcast_fusion.7), calls=%async_computation | async-start | bytes 262144 | tf_op jit(solution)/shard_map/all_to_all | solution.py:105
  47.5 12.4 %all-to-all-start.1 = ((bf16[64,8,128]{2,0,1:T(8,128)(2,1)}), bf16[64,8,128]{2,0,1:T(8,128)(2,1)S(1)}, u32[]{:S(2)}, u32[]{:S(2)}) async-start(bf16[64,8,128]{2,0,1:T(8,128)(2,1)} %copy_bitcast_fusion.6), calls=%async_computation.1 | async-start | bytes 262144 | tf_op jit(solution)/shard_map/all_to_all | solution.py:106
  59.9 12.4 %all-to-all-start.4 = ((bf16[64,8,128]{2,0,1:T(8,128)(2,1)}), bf16[64,8,128]{2,0,1:T(8,128)(2,1)S(1)}, u32[]{:S(2)}, u32[]{:S(2)}) async-start(bf16[64,8,128]{2,0,1:T(8,128)(2,1)} %copy_bitcast_fusion.5), calls=%async_computation.4 | async-start | bytes 262144 | tf_op jit(solution)/shard_map/all_to_all | solution.py:104
  72.3 12.4 %all-to-all-start.6 = ((bf16[64,8,128]{2,0,1:T(8,128)(2,1)}), bf16[64,8,128]{2,0,1:T(8,128)(2,1)S(1)}, u32[]{:S(2)}, u32[]{:S(2)}) async-start(bf16[64,8,128]{2,0,1:T(8,128)(2,1)} %copy_bitcast_fusion.4), calls=%async_computation.6 | async-start | bytes 262144 | tf_op jit(solution)/shard_map/all_to_all | solution.py:107
  77.3 13.4 %copy-start.11 = (s32[2]{0:T(128)S(1)}, s32[2]{0:T(128)}, u32[]{:S(2)}) copy-start(s32[2]{0:T(128)} %param.19) | copy-start | bytes 28
  84.7 195.6 %all-to-all-start.3 = ((bf16[64,1,64,256]{3,2,1,0:T(8,128)(2,1)}), bf16[64,1,64,256]{3,2,1,0:T(8,128)(2,1)S(1)}, u32[]{:S(2)}, u32[]{:S(2)}) async-start(bf16[64,1,64,256]{3,2,1,0:T(8,128)(2,1)} %fusion.9), calls=%async_computation.3 | async-start | bytes 4194304 | tf_op jit(solution)/shard_map/all_to_all | solution.py:141
  90.6 186.5 %all-reduce.7.cloned.1.call-start = ((), (), s32[]{:S(2)}) async-start(), calls=%async_computation.12 | async-start | bytes 131072 | tf_op jit(solution)/shard_map/psum | solution.py:29
  99.8 311.4 %all-gather.3.cloned.1.call-start = ((), (), s32[]{:S(2)}) async-start(), calls=%async_computation.11 | async-start | bytes 8519680 | tf_op jit(solution)/shard_map/all_gather | solution.py:212
  100.0 185.3 %copy-start.5 = (bf16[8,64,128]{1,2,0:T(8,128)(2,1)}, bf16[8,64,128]{1,2,0:T(8,128)(2,1)S(1)}, u32[]{:S(2)}) copy-start(bf16[8,64,128]{1,2,0:T(8,128)(2,1)S(1)} %copy.199) | copy-start | bytes 393220
  100.1 177.9 %collective-permute-start.1 = (bf16[64,256]{1,0:T(8,128)(2,1)S(1)}, bf16[64,256]{1,0:T(8,128)(2,1)S(1)}, u32[]{:S(2)}, u32[]{:S(2)}) collective-permute-start(bf16[64,256]{1,0:T(8,128)(2,1)S(1)} %get-tuple-element.103), channel_id=1, source_target_pairs={{8,0},{16,8},{24,16},{32,24},{40,32},{48,40},{56,48},{64,56},{72,6... | collective-permute-start | bytes 98312 | tf_op jit(solution)/shard_map/ppermute | solution.py:22
  102.1 175.9 %collective-permute-start = (bf16[64,256]{1,0:T(8,128)(2,1)S(1)}, bf16[64,256]{1,0:T(8,128)(2,1)S(1)}, u32[]{:S(2)}, u32[]{:S(2)}) collective-permute-start(bf16[64,256]{1,0:T(8,128)(2,1)S(1)} %get-tuple-element.104), channel_id=1, source_target_pairs={{0,8},{8,16},{16,24},{24,32},{32,40},{40,48},{48,56},{56,64},{64,7... | collective-permute-start | bytes 98312 | tf_op jit(solution)/shard_map/ppermute | solution.py:21
  284.8 2.7 copy-start.1
  285.3 5.1 %copy-start.3 = (bf16[8,448,128]{1,2,0:T(8,128)(2,1)}, bf16[8,448,128]{1,2,0:T(8,128)(2,1)S(1)}, u32[]{:S(2)}) copy-start(bf16[8,448,128]{1,2,0:T(8,128)(2,1)S(1)} %copy.170) | copy-start | bytes 2752516
  287.5 3.0 copy-start.12
  309.8 17.1 %all-to-all-start.5 = ((bf16[8,64,128]{2,1,0:T(8,128)(2,1)}), bf16[8,64,128]{2,1,0:T(8,128)(2,1)}, u32[]{:S(2)}, u32[]{:S(2)}) async-start(bf16[8,64,128]{2,1,0:T(8,128)(2,1)} %copy.174), calls=%async_computation.5 | async-start | bytes 262144 | tf_op jit(solution)/shard_map/all_to_all | solution.py:221
  327.0 88.2 %all-to-all-start.8 = ((bf16[64,1,64,256]{3,2,1,0:T(8,128)(2,1)}), bf16[64,1,64,256]{3,2,1,0:T(8,128)(2,1)}, u32[]{:S(2)}, u32[]{:S(2)}) async-start(bf16[64,1,64,256]{3,2,1,0:T(8,128)(2,1)} %fusion.5), calls=%async_computation.8 | async-start | bytes 4194304 | tf_op jit(solution)/shard_map/all_to_all | solution.py:203
  338.3 52.3 %collective-permute-start.2 = (bf16[64,256]{1,0:T(8,128)(2,1)S(1)}, bf16[64,256]{1,0:T(8,128)(2,1)S(1)}, u32[]{:S(2)}, u32[]{:S(2)}) collective-permute-start(bf16[64,256]{1,0:T(8,128)(2,1)S(1)} %get-tuple-element.96), channel_id=1, source_target_pairs={{8,0},{16,8},{24,16},{32,24},{40,32},{48,40},{56,48},{64,56},{72,6... | collective-permute-start | bytes 98312 | tf_op jit(solution)/shard_map/ppermute | solution.py:35
  341.7 49.2 %collective-permute-start.3 = (bf16[64,256]{1,0:T(8,128)(2,1)S(1)}, bf16[64,256]{1,0:T(8,128)(2,1)S(1)}, u32[]{:S(2)}, u32[]{:S(2)}) collective-permute-start(bf16[64,256]{1,0:T(8,128)(2,1)S(1)} %get-tuple-element.95), channel_id=1, source_target_pairs={{0,8},{8,16},{16,24},{24,32},{32,40},{40,48},{48,56},{56,64},{64,7... | collective-permute-start | bytes 98312 | tf_op jit(solution)/shard_map/ppermute | solution.py:35
  415.1 14.6 %all-to-all-start.7 = ((bf16[8,64,128]{2,1,0:T(8,128)(2,1)}), bf16[8,64,128]{2,1,0:T(8,128)(2,1)S(1)}, u32[]{:S(2)}, u32[]{:S(2)}) async-start(bf16[8,64,128]{2,1,0:T(8,128)(2,1)} %copy.179), calls=%async_computation.7 | async-start | bytes 262144 | tf_op jit(solution)/shard_map/all_to_all | solution.py:222
  429.7 12.4 %all-to-all-start.9 = ((bf16[8,64,128]{2,1,0:T(8,128)(2,1)}), bf16[8,64,128]{2,1,0:T(8,128)(2,1)S(1)}, u32[]{:S(2)}, u32[]{:S(2)}) async-start(bf16[8,64,128]{2,1,0:T(8,128)(2,1)} %bitcast.57), calls=%async_computation.9 | async-start | bytes 262144 | tf_op jit(solution)/shard_map/all_to_all | solution.py:223
  442.1 12.4 %all-to-all-start.10 = ((bf16[8,64,128]{2,1,0:T(8,128)(2,1)}), bf16[8,64,128]{2,1,0:T(8,128)(2,1)S(1)}, u32[]{:S(2)}, u32[]{:S(2)}) async-start(bf16[8,64,128]{2,1,0:T(8,128)(2,1)} %bitcast.59), calls=%async_computation.10 | async-start | bytes 262144 | tf_op jit(solution)/shard_map/all_to_all | solution.py:224
  (6 other events, 11.1 us)
Sparse Core Ops, SparseCore 0:
  99.9 177.2 all-reduce.6
  309.0 102.0 all-gather.2
